TPU v7x, 128 devices: a whole 4x4x4 slice. The times are simulated.
128 devices in a mesh: tm: 8 (over x, core), dp: 8 (over y, z_lo), group: 2 (over z_hi).
Axes of the slice: x: 4, y: 4, z: 4 (z_hi: 2, z_lo: 2; z = z_hi * 2 + z_lo), core: 2. Of those that a mesh axis runs over, the one named last changes fastest.
Arguments:
- features: bfloat16 [16, 32, 256, 2048], P(('dp', 'group'), 'tm'), may hold values from -6 to 6
- conv_weight: bfloat16 [3, 256, 256], replicated, may hold values from -0.21875 to 0.21875
- out_weight: bfloat16 [48, 256], replicated, may hold values from -0.375 to 0.375
- first_weight: bfloat16 [3, 256, 48], replicated, may hold values from -0.5 to 0.5
- second_weight: bfloat16 [3, 256, 256], replicated, may hold values from -0.21875 to 0.21875
- head_weight: bfloat16 [256], replicated, may hold values from -0.375 to 0.375
- span_lengths: int32 [16, 4], P(('dp', 'group')), may hold values from 1 to 16, 32 in all within a row
- labels: int32 [16], P(('dp', 'group')), may hold values 0 or 1
Outputs:
- conv_grad: float32 [3, 256, 256], replicated
- out_grad: float32 [48, 256], replicated
- first_grad: float32 [3, 256, 48], replicated
- second_grad: float32 [3, 256, 256], replicated
- head_grad: float32 [256], replicated
Inputs may be any that keep to these rules, and one draw needn't show every extreme that they name: `span_lengths`: each clip's 4 span lengths sum to 32; the longest is 16.
All inputs are finite; a program needn't handle non-finite values. No bound on the sum of `labels` on one device may be relied on, other than what follows from the above.
Results may differ from a plain program's by a relative error of at most 0.013.
The roundings to bfloat16 on the way count: a program that leaves them out, or rounds other values in their place, can miss the bound.
Values may be sent and summed in bfloat16 or wider, within the bound.
A program may use at most 192 MiB of HBM per device.

v0:
```python
import functools

import jax
import jax.numpy as jnp
from jax import lax
from jax.experimental import pallas as pl
from jax.experimental.pallas import tpu as pltpu
from jax.sharding import PartitionSpec as P

MESH = pl.DeviceIdType.MESH
F32 = jnp.float32


class Place:
    def __init__(self):
        tm, dp, group = (lax.axis_index(name) for name in ("tm", "dp", "group"))
        self.core = lax.rem(tm, 2)
        self.at = (tm // 2, dp // 2, 2 * group + lax.rem(dp, 2))

    def device(self, x, y, z, core):
        return (2 * x + core, 2 * y + lax.rem(z, 2), z // 2)

    def along(self, axis, step):
        place = list(self.at)
        place[axis] = lax.rem(place[axis] + step, 4)
        return self.device(*place, self.core)

    def other_core(self):
        return self.device(*self.at, 1 - self.core)


class Reducer:
    def __init__(self, place, grads, total, bufs, send_sems, recv_sems):
        self.place, self.grads, self.total = (place, grads, total)
        self.core_in, self.sum1, self.in1, self.sum2, self.in2, self.in3 = bufs
        self.send_sems, self.recv_sems = (send_sems, recv_sems)
        self.rows = grads.shape[1]
        self.sent = []
        self.axes = [tuple((part + i) % 3 for i in range(3)) for part in range(3)]

    def copy(self, src, dst, slot, device):
        return pltpu.make_async_remote_copy(
            src_ref=src,
            dst_ref=dst,
            send_sem=self.send_sems.at[slot],
            recv_sem=self.recv_sems.at[slot],
            device_id=device,
            device_id_type=MESH,
        )

    def start(self, *args):
        copy = self.copy(*args)
        copy.start()
        self.sent.append(copy)

    def lanes(self, core):
        return pl.ds(pl.multiple_of(core * 128, 128), 128)

    def block(self, index, size):
        return pl.ds(pl.multiple_of(index * size, size), size)

    def slot(self, stage, part, step):
        return 3 + (stage * 3 + part) * 3 + step - 1

    def core_send(self, part):
        place = self.place
        src = self.grads.at[part, :, self.lanes(1 - place.core)]
        self.start(src, self.core_in.at[part], part, place.other_core())

    def core_sum(self, part):
        place = self.place
        self.copy(self.core_in.at[part], self.core_in.at[part], part, place.other_core()).wait_recv()
        self.sum1[part] = self.grads[part, :, self.lanes(place.core)] + self.core_in[part]

    def scatter_send(self, part, level):
        axis = self.axes[part][level]
        source, landing = ((self.sum1, self.in1), (self.sum2, self.in2))[level]
        size = landing.shape[2]
        for step in (1, 2, 3):
            target = lax.rem(self.place.at[axis] + step, 4)
            self.start(
                source.at[part, self.block(target, size)],
                landing.at[part, step - 1],
                self.slot(level, part, step),
                self.place.along(axis, step),
            )

    def scatter_sum(self, part, level):
        axis = self.axes[part][level]
        source, landing = ((self.sum1, self.in1), (self.sum2, self.in2))[level]
        size = landing.shape[2]
        for step in (1, 2, 3):
            here = landing.at[part, step - 1]
            self.copy(here, here, self.slot(level, part, step), self.place.along(axis, step)).wait_recv()
        result = source[part, self.block(self.place.at[axis], size)]
        for step in (1, 2, 3):
            result = result + landing[part, step - 1]
        if level == 0:
            self.sum2[part] = result
        else:
            self.in3[part, self.place.at[self.axes[part][2]]] = result

    def swap_send(self, part):
        axis = self.axes[part][2]
        here = self.in3.at[part, self.place.at[axis]]
        for step in (1, 2, 3):
            self.start(here, here, self.slot(2, part, step), self.place.along(axis, step))

    def rows_of(self, part, level):
        first = self.place.at[self.axes[part][0]]
        if level == 0:
            return self.block(first, self.rows // 4)
        return self.block(4 * first + self.place.at[self.axes[part][1]], self.rows // 16)

    def swap_sum(self, part):
        axis = self.axes[part][2]
        for step in (1, 2, 3):
            here = self.in3.at[part, step]
            self.copy(here, here, self.slot(2, part, step), self.place.along(axis, step)).wait_recv()
        result = (self.in3[part, 0] + self.in3[part, 1]) + (self.in3[part, 2] + self.in3[part, 3])
        self.total[part, self.rows_of(part, 1), self.lanes(self.place.core)] = result.astype(self.total.dtype)

    def gather_send(self, part, level):
        axis = self.axes[part][level]
        here = self.total.at[part, self.rows_of(part, level), self.lanes(self.place.core)]
        for step in (1, 2, 3):
            self.start(here, here, self.slot(4 - level, part, step), self.place.along(axis, step))

    def gather_wait(self, part, level):
        axis = self.axes[part][level]
        here = self.total.at[part, self.rows_of(part, level), self.lanes(self.place.core)]
        for step in (1, 2, 3):
            self.copy(here, here, self.slot(4 - level, part, step), self.place.along(axis, step)).wait_recv()

    def back_send(self, part):
        here = self.total.at[part, :, self.lanes(self.place.core)]
        self.start(here, here, 48 + part, self.place.other_core())

    def back_wait(self, part):
        here = self.total.at[part, :, self.lanes(1 - self.place.core)]
        self.copy(here, here, 48 + part, self.place.other_core()).wait_recv()

    def steps(self):
        def each(*calls):
            def run():
                for part in range(3):
                    for call, *level in calls:
                        call(part, *level)

            return run

        return [
            each((self.core_send,)),
            each((self.core_sum,), (self.scatter_send, 0)),
            each((self.scatter_sum, 0), (self.scatter_send, 1)),
            each((self.scatter_sum, 1), (self.swap_send,)),
            each((self.swap_sum,), (self.gather_send, 1)),
            each((self.gather_wait, 1), (self.gather_send, 0)),
            each((self.gather_wait, 0), (self.back_send,)),
            each((self.back_wait,)),
        ]

    def finish(self):
        for copy in self.sent:
            copy.wait_send()


N_SLOTS = 51


def reduce_scratch(rows):
    return [
        pltpu.VMEM((3, rows, 128), F32),
        pltpu.VMEM((3, rows, 128), F32),
        pltpu.VMEM((3, 3, rows // 4, 128), F32),
        pltpu.VMEM((3, rows // 4, 128), F32),
        pltpu.VMEM((3, 3, rows // 16, 128), F32),
        pltpu.VMEM((3, 4, rows // 16, 128), F32),
    ]


SC = 256
WIDTH = 1024
NCH = WIDTH // SC
MIB = 1024 * 1024


def dot(a, b):
    return jnp.dot(a, b, preferred_element_type=F32)


def dot_nt(a, b):
    return lax.dot_general(a, b, (((1,), (1,)), ((), ())), preferred_element_type=F32)


def rows_at(frame, height, count=1):
    start = frame * height
    return pl.ds(start if isinstance(start, int) else pl.multiple_of(start, height), height * count)


def frame_loop(low, high, group, body):
    count = (high - low) // group
    if count == 1:
        for frame in range(low, high):
            body(frame)
        return

    def step(index, carry):
        for offset in range(group):
            body(low + index * group + offset)
        return carry

    lax.fori_loop(0, count, step, 0)


def block_kernel(
    loss_scale,
    spans, labels, feat, cw, ow, owt, fw, fwt, sw, swt, head,
    total1, total2,
    frames, hidden, slopes, recon, disc, second, first, parts, rgrad, masked,
    acc_conv, acc_second, acc_first, acc_out, acc_head, grads1, grads2,
    own_sem, core_send, core_recv, halo_send, halo_recv, low_send, low_recv, high_send, high_recv,
    send1, recv1, send2, recv2, *bufs,
):
    place = Place()
    x, y, z = place.at
    core = place.core
    clip_start, clip_end = x == 0, x == 3
    inner_low, inner_high = x > 0, x < 3

    def cols(chunk, base=0):
        return pl.ds(pl.multiple_of(base + chunk * SC, SC), SC)

    def own_copy(chunk):
        return pltpu.make_async_copy(
            feat.at[:, cols(chunk, core * WIDTH)],
            frames.at[rows_at(2 + 4 * core, 256, 4), cols(chunk)],
            own_sem.at[chunk],
        )

    def remote(src, dst, send, recv, device):
        return pltpu.make_async_remote_copy(
            src_ref=src, dst_ref=dst, send_sem=send, recv_sem=recv, device_id=device, device_id_type=MESH
        )

    def core_copy(chunk):
        return remote(
            feat.at[:, cols(chunk, (1 - core) * WIDTH)],
            frames.at[rows_at(2 + 4 * core, 256, 4), cols(chunk)],
            core_send.at[chunk],
            core_recv.at[chunk],
            place.other_core(),
        )

    def halo_copy(chunk, target):
        return remote(
            feat.at[512:1024, cols(chunk, target * WIDTH)],
            frames.at[0:512, cols(chunk)],
            halo_send.at[chunk, target],
            halo_recv.at[chunk],
            place.device(x + 1, y, z, target),
        )

    def low_copy(chunk):
        return remote(
            recon.at[384:576, cols(chunk)],
            recon.at[0:192, cols(chunk)],
            low_send.at[chunk],
            low_recv.at[chunk],
            place.device(x + 1, y, z, core),
        )

    def high_copy(chunk):
        return remote(
            recon.at[192:384, cols(chunk)],
            recon.at[576:768, cols(chunk)],
            high_send.at[chunk],
            high_recv.at[chunk],
            place.device(x - 1, y, z, core),
        )

    for chunk in range(NCH):
        own_copy(chunk).start()

    barrier = pltpu.get_barrier_semaphore()
    partners = [place.other_core()] + [place.along(axis, step) for axis in range(3) for step in (1, 2, 3)]
    partners += [place.device(lax.rem(x + step, 4), y, z, 1 - core) for step in (1, 3)]
    for device in partners:
        pl.semaphore_signal(barrier, inc=1, device_id=device, device_id_type=MESH)
    pl.semaphore_wait(barrier, len(partners))

    for chunk in range(NCH):
        core_copy(chunk).start()

    @pl.when((core == 1) & inner_high)
    def _():
        for chunk in range(NCH):
            for target in (0, 1):
                halo_copy(chunk, target).start()

    @pl.when(clip_start)
    def _():
        frames[0:512] = jnp.zeros((512, WIDTH), jnp.bfloat16)
        recon[0:192] = jnp.zeros((192, WIDTH), jnp.bfloat16)

    @pl.when(clip_end)
    def _():
        recon[576:768] = jnp.zeros((192, WIDTH), jnp.bfloat16)

    ends = []
    for span in range(4):
        ends.append(spans[0, span] + (ends[-1] if ends else 0))

    def span_of(frame):
        return sum((frame >= end).astype(jnp.int32) for end in ends)

    def tap_mask(local, tap):
        frame = 8 * x + local
        same = (span_of(frame) == span_of(frame - tap)) & (frame >= tap)
        return jnp.where(same, 1.0, 0.0).astype(F32)

    def valid(local):
        frame = 8 * x + local
        return jnp.where((frame >= 0) & (frame < 32), 1.0, 0.0).astype(F32)

    def mask_weights(local, carry):
        rows = rows_at(local, 256)
        for place_of, tap in ((0, 2), (1, 1)):
            lanes = slice(256 * place_of, 256 * place_of + 256)
            weight = cw[:, lanes].astype(F32) * tap_mask(local, tap)
            masked[rows, lanes] = weight.astype(jnp.bfloat16)
        masked[rows, 512:768] = cw[:, 512:768]
        return carry

    lax.fori_loop(0, 8, mask_weights, 0)
    for acc in (acc_conv, acc_second, acc_first, acc_out, acc_head):
        acc[...] = jnp.zeros_like(acc)

    sign = (2 * labels[0] - 1).astype(F32)

    def decode(local, where):
        pre = dot(masked[rows_at(local, 256)], frames[rows_at(local, 256, 3), where])
        gate = 0.5 * jnp.tanh(0.5 * pre) + 0.5
        silu = pre * gate
        value = (frames[rows_at(local + 2, 256), where].astype(F32) + silu).astype(jnp.bfloat16)
        hidden[rows_at(local, 256), where] = value
        slopes[rows_at(local, 256), where] = gate + silu * (1.0 - gate)
        recon[rows_at(local + 4, 48), where] = dot(ow[...], value).astype(jnp.bfloat16)

    def decode_inner(chunk, carry):
        own_copy(chunk).wait()
        core_copy(chunk).wait_recv()
        frame_loop(2, 8, 3, lambda local: decode(local, cols(chunk)))
        return carry

    def decode_halo(chunk):
        @pl.when(inner_low)
        def _():
            halo_copy(chunk, 0).wait_recv()

        decode(0, cols(chunk))
        decode(1, cols(chunk))

        @pl.when(inner_high)
        def _():
            low_copy(chunk).start()

        @pl.when(inner_low)
        def _():
            high_copy(chunk).start()

    def first_layer(local, where):
        pre = dot(fw[...], recon[rows_at(local + 3, 48, 3), where])
        on = valid(local)
        value = pre * jnp.where(pre > 0, on, 0.2 * on)
        disc[rows_at(local + 3, 256)] = value.astype(jnp.bfloat16)

    def second_layer(local, own):
        pre = dot(sw[...], disc[rows_at(local + 2, 256, 3)])
        act = jnp.maximum(pre, 0.2 * pre)
        logits = jnp.sum(act * head[...], axis=0, keepdims=True)
        grad = (-sign * loss_scale * valid(local)) / (1.0 + jnp.exp(sign * logits))
        if own:
            term = act * grad
            acc_head[...] += sum(term[:, i : i + 128] for i in range(0, SC, 128))
        delta = head[...] * grad
        second[rows_at(local + 2, 256)] = jnp.where(pre > 0, delta, 0.2 * delta).astype(jnp.bfloat16)

    def first_back(local):
        back = dot(swt[...], second[rows_at(local + 1, 256, 3)])
        on = valid(local)
        slope = jnp.where(disc[rows_at(local + 3, 256)].astype(F32) > 0, on, 0.2 * on)
        value = (back * slope).astype(jnp.bfloat16)
        first[rows_at(local + 1, 256)] = value
        parts[rows_at(local + 1, 144)] = dot(fwt[...], value)

    def recon_back(local, where):
        total = (
            parts[pl.ds((local + 2) * 144, 48)]
            + parts[pl.ds((local + 1) * 144 + 48, 48)]
            + parts[pl.ds(local * 144 + 96, 48)]
        )
        rgrad[rows_at(local, 48), where] = total.astype(jnp.bfloat16)

    def wide(ref, starts, count, where=slice(None)):
        return jnp.concatenate([ref[start : start + count, where] for start in starts], axis=1)

    def weight_grads(where):
        own = range(8)
        acc_second[...] += dot_nt(
            wide(disc, [(t + 2) * 256 for t in own], 768), wide(second, [(t + 2) * 256 for t in own], 256)
        )
        acc_first[...] += dot_nt(
            wide(recon, [(t + 3) * 48 for t in own], 144, where), wide(first, [(t + 1) * 256 for t in own], 256)
        )
        acc_out[...] += dot_nt(
            wide(rgrad, [t * 48 for t in own], 48, where), wide(hidden, [t * 256 for t in own], 256, where)
        )

    lax.fori_loop(0, NCH - 1, decode_inner, 0)
    decode_halo(0)
    decode_inner(NCH - 1, 0)

    def chunk_step(chunk, carry):
        where = cols(chunk)

        @pl.when(inner_low)
        def _():
            low_copy(chunk).wait_recv()

        @pl.when(inner_high)
        def _():
            high_copy(chunk).wait_recv()

        frame_loop(-3, 11, 7, lambda local: first_layer(local, where))
        frame_loop(-2, 0, 2, lambda local: second_layer(local, False))
        frame_loop(0, 8, 4, lambda local: second_layer(local, True))
        frame_loop(8, 10, 2, lambda local: second_layer(local, False))
        frame_loop(-1, 9, 5, first_back)
        for local in range(8):
            recon_back(local, where)

        @pl.when(chunk < NCH - 1)
        def _():
            decode_halo(chunk + 1)

        weight_grads(where)
        return carry

    lax.fori_loop(0, NCH, chunk_step, 0)

    for part in range(3):
        grads1[part, 0:256] = acc_second[256 * part : 256 * part + 256].T
        grads1[part, 256:304] = acc_first[48 * part : 48 * part + 48]
        grads1[part, 304:320] = acc_out[16 * part : 16 * part + 16]
        grads1[part, 320:384] = jnp.zeros((64, 256), F32)
    grads1[0, 320:328] = jnp.broadcast_to(jnp.sum(acc_head[...].T, axis=0, keepdims=True), (8, 256))

    reduce1 = Reducer(place, grads1, total1, bufs[:6], send1, recv1)
    reduce2 = Reducer(place, grads2, total2, bufs[6:], send2, recv2)
    steps1, steps2 = reduce1.steps(), reduce2.steps()

    def conv_back(local):
        back = dot(owt[...], rgrad[rows_at(local, 48)])
        delta = (back * slopes[rows_at(local, 256)]).astype(jnp.bfloat16)
        result = dot_nt(frames[rows_at(local, 256, 3)], delta)
        for block, tap in ((0, 2), (1, 1), (2, 0)):
            rows = slice(256 * block, 256 * block + 256)
            acc_conv[rows] += result[rows] * tap_mask(local, tap)

    steps1[0]()
    for pair in range(4):
        lax.fori_loop(2 * pair, 2 * pair + 2, lambda local, carry: (conv_back(local), carry)[1], 0)
        if pair < 3:
            steps1[pair + 1]()
    for tap in range(3):
        grads2[tap] = acc_conv[256 * (2 - tap) : 256 * (2 - tap) + 256].T
    steps2[0]()
    for index in range(4, 8):
        steps1[index]()
        steps2[index - 3]()
    for index in range(5, 8):
        steps2[index]()

    reduce1.finish()
    reduce2.finish()
    for chunk in range(NCH):
        core_copy(chunk).wait_send()

        @pl.when((core == 1) & inner_high)
        def _():
            halo_copy(chunk, 0).wait_send()
            halo_copy(chunk, 1).wait_send()

        @pl.when(inner_high)
        def _():
            low_copy(chunk).wait_send()

        @pl.when(inner_low)
        def _():
            high_copy(chunk).wait_send()


def per_device(
    features, conv_weight, out_weight, first_weight, second_weight, head_weight, span_lengths, labels
):
    clips, frame_count, channels, positions = features.shape
    total_count = (
        clips * lax.axis_size("dp") * lax.axis_size("group") * frame_count * lax.axis_size("tm") * positions
    )
    loss_scale = float(total_count) ** (-0.5)
    bf16 = jnp.bfloat16
    operands = (
        span_lengths,
        labels,
        features.reshape(frame_count * channels, positions),
        jnp.concatenate([conv_weight[2], conv_weight[1], conv_weight[0]], axis=1),
        out_weight,
        out_weight.T,
        jnp.concatenate([first_weight[0], first_weight[1], first_weight[2]], axis=1),
        jnp.swapaxes(first_weight, 1, 2).reshape(144, 256),
        jnp.concatenate([second_weight[0], second_weight[1], second_weight[2]], axis=1),
        jnp.concatenate([second_weight[2].T, second_weight[1].T, second_weight[0].T], axis=1),
        jnp.broadcast_to(head_weight.astype(F32)[:, None], (256, SC)),
    )
    smem, vmem = pl.BlockSpec(memory_space=pltpu.SMEM), pl.BlockSpec(memory_space=pltpu.VMEM)
    dma = pltpu.SemaphoreType.DMA
    total1, total2 = pl.pallas_call(
        functools.partial(block_kernel, loss_scale),
        out_shape=(
            jax.ShapeDtypeStruct((3, 384, 256), F32),
            jax.ShapeDtypeStruct((3, 256, 256), F32),
        ),
        in_specs=[smem, smem, pl.BlockSpec(memory_space=pl.ANY)] + [vmem] * 8,
        out_specs=(vmem, vmem),
        scratch_shapes=[
            pltpu.VMEM((2560, WIDTH), bf16),
            pltpu.VMEM((2048, WIDTH), bf16),
            pltpu.VMEM((2048, WIDTH), F32),
            pltpu.VMEM((768, WIDTH), bf16),
            pltpu.VMEM((14 * 256, SC), bf16),
            pltpu.VMEM((12 * 256, SC), bf16),
            pltpu.VMEM((10 * 256, SC), bf16),
            pltpu.VMEM((10 * 144, SC), F32),
            pltpu.VMEM((8 * 48, WIDTH), bf16),
            pltpu.VMEM((2048, 768), bf16),
            pltpu.VMEM((768, 256), F32),
            pltpu.VMEM((768, 256), F32),
            pltpu.VMEM((144, 256), F32),
            pltpu.VMEM((48, 256), F32),
            pltpu.VMEM((256, 128), F32),
            pltpu.VMEM((3, 384, 256), F32),
            pltpu.VMEM((3, 256, 256), F32),
            dma((NCH,)),
            dma((NCH,)),
            dma((NCH,)),
            dma((NCH, 2)),
            dma((NCH,)),
            dma((NCH,)),
            dma((NCH,)),
            dma((NCH,)),
            dma((NCH,)),
            dma((N_SLOTS,)),
            dma((N_SLOTS,)),
            dma((N_SLOTS,)),
            dma((N_SLOTS,)),
        ]
        + reduce_scratch(384)
        + reduce_scratch(256),
        compiler_params=pltpu.CompilerParams(
            collective_id=0, has_side_effects=True, vmem_limit_bytes=56 * MIB
        ),
    )(*operands)
    return (
        total2,
        total1[:, 304:320].reshape(48, 256),
        jnp.swapaxes(total1[:, 256:304], 1, 2),
        total1[:, 0:256],
        total1[0, 320],
    )


def solution(mesh):
    placed = (
        P(("dp", "group"), "tm", None, None),
        P(),
        P(),
        P(),
        P(),
        P(),
        P(("dp", "group"), None),
        P(("dp", "group")),
    )
    return jax.shard_map(
        per_device, mesh=mesh, in_specs=placed, out_specs=(P(), P(), P(), P(), P()), check_vma=False
    )
```

profile of v0, /device:TPU:1, one launch (start us, length us, event | category | flops | bytes accessed | tf_op | source)
XLA Modules:
  0.0 135.7 jit_solution(10105672041531570391)
XLA Ops:
  0.6 0.0 copy-start.2
  0.6 0.0 copy-start.1
  1.4 1.5 %copy.13 = bf16[48,256]{0,1:T(8,128)(2,1)} copy(bf16[48,256]{1,0:T(8,128)(2,1)} %ow.1) | data formatting | bytes 49152 | tf_op args[2]
  2.8 0.8 fusion.1
  3.6 0.1 copy.21
  3.7 0.1 copy.22
  3.8 0.1 copy.23
  4.0 0.8 pad_maximum_fusion.3.fw
  4.8 1.5 %broadcast_in_dim.2.head = f32[256,256]{1,0:T(8,128)} broadcast(bf16[256]{0:T(256)(128)(2,1)} %param.13), dimensions={0} | broadcast | bytes 262656 | tf_op jit(solution)/shard_map/broadcast_in_dim | solution.py:524
  6.2 0.0 copy-done.1
  6.3 0.0 copy-done.2
  6.3 0.1 copy.24
  6.4 0.1 copy.25
  6.5 0.1 copy.26
  6.7 0.9 copy.20.sw
  7.6 0.9 pad_maximum_fusion
  8.5 119.9 %shard_map.119 = (f32[3,384,256]{2,1,0:T(8,128)}, f32[3,256,256]{2,1,0:T(8,128)}) custom-call(s32[1,4]{1,0:T(1,128)} %spans.1, s32[1]{0:T(128)S(6)} %copy.28.labels, bf16[1024,2048]{1,0:T(8,128)(2,1)} %bitcast.27, bf16[256,768]{1,0:T(8,128)(2,1)} %get-tuple-element.18.cw, bf16[48,256]{1,0:T(8,128)(2,1)} %ow.1, bf16[256,48]{1,0:T(8,128)(2,1)} %bitcast.35, ...), custom_call_target="tpu_custom_call" | custom-call | tf_op jit(solution)/shard_map/pallas_call | solution.py:528
  128.4 0.0 copy-start
  128.4 1.3 slice.54
  129.8 1.4 %slice.51 = f32[3,16,256]{2,1,0:T(8,128)} slice(f32[3,384,256]{2,1,0:T(8,128)} %get-tuple-element.8), slice={[0:3], [304:320], [0:256]} | slice | bytes 98304 | tf_op jit(solution)/shard_map/slice | solution.py:576
  131.2 1.6 %slice_bitcast_fusion = f32[3,256,48]{1,2,0:T(8,128)} fusion(f32[3,384,256]{2,1,0:T(8,128)} %get-tuple-element.8), kind=kLoop, calls=%fused_computation.3 | loop fusion | bytes 294912 | tf_op jit(solution)/shard_map/transpose | solution.py:577
  132.8 2.1 %slice.53 = f32[3,256,256]{2,1,0:T(8,128)} slice(f32[3,384,256]{2,1,0:T(8,128)} %get-tuple-element.8), slice={[0:3], [0:256], [0:256]} | slice | bytes 1572864 | tf_op jit(solution)/shard_map/slice | solution.py:578
  134.8 0.0 copy-done
  134.8 0.9 copy.29
  (3 shorter events, 0.1 us)
Async XLA Ops:
  0.6 5.6 %copy-start.2 = (bf16[3,256,256]{2,1,0:T(8,128)(2,1)S(1)}, bf16[3,256,256]{2,1,0:T(8,128)(2,1)}, u32[]{:S(2)}) copy-start(bf16[3,256,256]{2,1,0:T(8,128)(2,1)} %param.12) | copy-start | bytes 1179652
  0.6 5.6 %copy-start.1 = (bf16[3,256,256]{2,1,0:T(8,128)(2,1)S(1)}, bf16[3,256,256]{2,1,0:T(8,128)(2,1)}, u32[]{:S(2)}) copy-start(bf16[3,256,256]{2,1,0:T(8,128)(2,1)} %param.9) | copy-start | bytes 1179652
  128.4 6.4 %copy-start = (f32[3,256,256]{2,1,0:T(8,128)S(1)}, f32[3,256,256]{2,1,0:T(8,128)}, u32[]{:S(2)}) copy-start(f32[3,256,256]{2,1,0:T(8,128)} %get-tuple-element.25) | copy-start | bytes 2359300
where the time goes:
time: 136 us
  Pallas kernels  120 us (88%)
  local copies, waits for them, and re-layouts  12.6 us (9%)
  other arithmetic  1.76 us (1%)
  between operations  1.45 us (1%)
    pallas_call x1, Pallas kernels, per_device(): pl.pallas_call(functools.partial(block_kernel, loss_scale), out_shape=(ja...  120 us
    unnamed x14, local copies, waits for them, and re-layouts  2.99 us

commit v1 on v0

--- a/solution.py
+++ b/solution.py
@@ -179,7 +179,7 @@
     ]
 
 
-SC = 256
+SC = 512
 WIDTH = 1024
 NCH = WIDTH // SC
 MIB = 1024 * 1024
@@ -198,25 +198,11 @@
     return pl.ds(start if isinstance(start, int) else pl.multiple_of(start, height), height * count)
 
 
-def frame_loop(low, high, group, body):
-    count = (high - low) // group
-    if count == 1:
-        for frame in range(low, high):
-            body(frame)
-        return
-
-    def step(index, carry):
-        for offset in range(group):
-            body(low + index * group + offset)
-        return carry
-
-    lax.fori_loop(0, count, step, 0)
-
-
 def block_kernel(
     loss_scale,
-    spans, labels, feat, cw, ow, owt, fw, fwt, sw, swt, head,
-    total1, total2,
+    spans, labels, feat, conv_w, ow, fwt, second_w, head_w,
+    conv_out, out_out, first_out, second_out, head_out,
+    owt, fw, sw, swt, head, total1, total2,
     frames, hidden, slopes, recon, disc, second, first, parts, rgrad, masked,
     acc_conv, acc_second, acc_first, acc_out, acc_head, grads1, grads2,
     own_sem, core_send, core_recv, halo_send, halo_recv, low_send, low_recv, high_send, high_recv,
@@ -325,14 +311,27 @@
 
     def mask_weights(local, carry):
         rows = rows_at(local, 256)
-        for place_of, tap in ((0, 2), (1, 1)):
-            lanes = slice(256 * place_of, 256 * place_of + 256)
-            weight = cw[:, lanes].astype(F32) * tap_mask(local, tap)
-            masked[rows, lanes] = weight.astype(jnp.bfloat16)
-        masked[rows, 512:768] = cw[:, 512:768]
+        for block, tap in ((0, 2), (1, 1)):
+            weight = conv_w[tap].astype(F32) * tap_mask(local, tap)
+            masked[rows, 256 * block : 256 * block + 256] = weight.astype(jnp.bfloat16)
+        masked[rows, 512:768] = conv_w[0]
         return carry
 
+    def place_weights():
+        row, column = (lax.broadcasted_iota(jnp.int32, (256, 256), axis) for axis in (0, 1))
+        same = jnp.where(row == column, 1.0, 0.0).astype(jnp.bfloat16)
+        owt[...] = dot_nt(same, ow[...]).astype(jnp.bfloat16)
+        fw[...] = dot_nt(same, fwt[...]).astype(jnp.bfloat16)
+        for tap in range(3):
+            sw[:, 256 * tap : 256 * tap + 256] = second_w[tap]
+            turned = dot_nt(same, second_w[tap]).astype(jnp.bfloat16)
+            swt[:, 512 - 256 * tap : 768 - 256 * tap] = turned
+        row = jnp.broadcast_to(head_w[...].astype(F32), (256, 256)).astype(jnp.bfloat16)
+        column = dot_nt(same, row)
+        head[...] = jnp.concatenate([column] * (SC // 256), axis=1)
+
     lax.fori_loop(0, 8, mask_weights, 0)
+    place_weights()
     for acc in (acc_conv, acc_second, acc_first, acc_out, acc_head):
         acc[...] = jnp.zeros_like(acc)
 
@@ -347,11 +346,11 @@
         slopes[rows_at(local, 256), where] = gate + silu * (1.0 - gate)
         recon[rows_at(local + 4, 48), where] = dot(ow[...], value).astype(jnp.bfloat16)
 
-    def decode_inner(chunk, carry):
+    def decode_inner(chunk):
         own_copy(chunk).wait()
         core_copy(chunk).wait_recv()
-        frame_loop(2, 8, 3, lambda local: decode(local, cols(chunk)))
-        return carry
+        for local in range(2, 8):
+            decode(local, cols(chunk))
 
     def decode_halo(chunk):
         @pl.when(inner_low)
@@ -417,11 +416,11 @@
             wide(rgrad, [t * 48 for t in own], 48, where), wide(hidden, [t * 256 for t in own], 256, where)
         )
 
-    lax.fori_loop(0, NCH - 1, decode_inner, 0)
+    for chunk in range(NCH):
+        decode_inner(chunk)
     decode_halo(0)
-    decode_inner(NCH - 1, 0)
-
-    def chunk_step(chunk, carry):
+
+    for chunk in range(NCH):
         where = cols(chunk)
 
         @pl.when(inner_low)
@@ -432,22 +431,19 @@
         def _():
             high_copy(chunk).wait_recv()
 
-        frame_loop(-3, 11, 7, lambda local: first_layer(local, where))
-        frame_loop(-2, 0, 2, lambda local: second_layer(local, False))
-        frame_loop(0, 8, 4, lambda local: second_layer(local, True))
-        frame_loop(8, 10, 2, lambda local: second_layer(local, False))
-        frame_loop(-1, 9, 5, first_back)
-        for local in range(8):
-            recon_back(local, where)
-
-        @pl.when(chunk < NCH - 1)
-        def _():
+        for step in range(-3, 14):
+            if step < 11:
+                first_layer(step, where)
+            if -2 <= step - 2 < 10:
+                second_layer(step - 2, 0 <= step - 2 < 8)
+            if -1 <= step - 4 < 9:
+                first_back(step - 4)
+            if 0 <= step - 6:
+                recon_back(step - 6, where)
+
+        if chunk + 1 < NCH:
             decode_halo(chunk + 1)
-
         weight_grads(where)
-        return carry
-
-    lax.fori_loop(0, NCH, chunk_step, 0)
 
     for part in range(3):
         grads1[part, 0:256] = acc_second[256 * part : 256 * part + 256].T
@@ -470,7 +466,8 @@
 
     steps1[0]()
     for pair in range(4):
-        lax.fori_loop(2 * pair, 2 * pair + 2, lambda local, carry: (conv_back(local), carry)[1], 0)
+        conv_back(2 * pair)
+        conv_back(2 * pair + 1)
         if pair < 3:
             steps1[pair + 1]()
     for tap in range(3):
@@ -481,6 +478,13 @@
         steps2[index - 3]()
     for index in range(5, 8):
         steps2[index]()
+
+    for part in range(3):
+        conv_out[part] = total2[part].astype(F32)
+        second_out[part] = total1[part, 0:256]
+        first_out[part] = total1[part, 256:304]
+        out_out[16 * part : 16 * part + 16] = total1[part, 304:320]
+    head_out[...] = total1[0, 320:321]
 
     reduce1.finish()
     reduce2.finish()
@@ -514,26 +518,33 @@
         span_lengths,
         labels,
         features.reshape(frame_count * channels, positions),
-        jnp.concatenate([conv_weight[2], conv_weight[1], conv_weight[0]], axis=1),
+        conv_weight,
         out_weight,
-        out_weight.T,
-        jnp.concatenate([first_weight[0], first_weight[1], first_weight[2]], axis=1),
         jnp.swapaxes(first_weight, 1, 2).reshape(144, 256),
-        jnp.concatenate([second_weight[0], second_weight[1], second_weight[2]], axis=1),
-        jnp.concatenate([second_weight[2].T, second_weight[1].T, second_weight[0].T], axis=1),
-        jnp.broadcast_to(head_weight.astype(F32)[:, None], (256, SC)),
+        second_weight,
+        head_weight.reshape(1, 256),
     )
     smem, vmem = pl.BlockSpec(memory_space=pltpu.SMEM), pl.BlockSpec(memory_space=pltpu.VMEM)
     dma = pltpu.SemaphoreType.DMA
-    total1, total2 = pl.pallas_call(
+    conv, out, first, second, head = pl.pallas_call(
         functools.partial(block_kernel, loss_scale),
         out_shape=(
-            jax.ShapeDtypeStruct((3, 384, 256), F32),
             jax.ShapeDtypeStruct((3, 256, 256), F32),
+            jax.ShapeDtypeStruct((48, 256), F32),
+            jax.ShapeDtypeStruct((3, 48, 256), F32),
+            jax.ShapeDtypeStruct((3, 256, 256), F32),
+            jax.ShapeDtypeStruct((1, 256), F32),
         ),
-        in_specs=[smem, smem, pl.BlockSpec(memory_space=pl.ANY)] + [vmem] * 8,
-        out_specs=(vmem, vmem),
+        in_specs=[smem, smem, pl.BlockSpec(memory_space=pl.ANY)] + [vmem] * 5,
+        out_specs=(vmem,) * 5,
         scratch_shapes=[
+            pltpu.VMEM((256, 48), bf16),
+            pltpu.VMEM((256, 144), bf16),
+            pltpu.VMEM((256, 768), bf16),
+            pltpu.VMEM((256, 768), bf16),
+            pltpu.VMEM((256, SC), F32),
+            pltpu.VMEM((3, 384, 256), F32),
+            pltpu.VMEM((3, 256, 256), bf16),
             pltpu.VMEM((2560, WIDTH), bf16),
             pltpu.VMEM((2048, WIDTH), bf16),
             pltpu.VMEM((2048, WIDTH), F32),
@@ -571,13 +582,7 @@
             collective_id=0, has_side_effects=True, vmem_limit_bytes=56 * MIB
         ),
     )(*operands)
-    return (
-        total2,
-        total1[:, 304:320].reshape(48, 256),
-        jnp.swapaxes(total1[:, 256:304], 1, 2),
-        total1[:, 0:256],
-        total1[0, 320],
-    )
+    return conv, out, jnp.swapaxes(first, 1, 2), second, head.reshape(256)
 
 
 def solution(mesh):

time: 136 us -> 116 us (0.85)
  Pallas kernels: 120 us -> 104 us
  local copies, waits for them, and re-layouts: 12.6 us -> 9.55 us
  other arithmetic: 1.76 us -> 0 us
    pallas_call x1, Pallas kernels: 120 us -> 104 us  [per_device(): pl.pallas_call(functools.partial(block_kernel, loss_scale), out_shape=(ja...]
    slice x5 -> x0, local copies, waits for them, and re-layouts: 5.62 us -> none  [the longest x1 2.06 us: per_device(): total1[:, 0:256]]
    unnamed x14 -> x5, local copies, waits for them, and re-layouts: 2.99 us -> 8.32 us
    concatenate x3 -> x0, other arithmetic: 1.76 us -> none  [the longest x1 0.93 us: per_device(): jnp.concatenate([conv_weight[2], conv_weight[1], conv_weight[0]], axis=1)]
    transpose x1 -> x0, local copies, waits for them, and re-layouts: 1.58 us -> none  [per_device(): jnp.swapaxes(total1[:, 256:304], 1, 2)]
    broadcast_in_dim x1 -> x0, local copies, waits for them, and re-layouts: 1.46 us -> none  [per_device(): jnp.broadcast_to(head_weight.astype(F32)[:, None], (256, SC))]
where the time goes in v1:
time: 116 us; the launch traced here: 115 us
  Pallas kernels  104 us (90%)
  local copies, waits for them, and re-layouts  9.55 us (8%)
  between operations  1.29 us (1%)
    pallas_call x1, Pallas kernels, per_device(): pl.pallas_call(functools.partial(block_kernel, loss_scale), out_shape=(ja...  104 us
    unnamed x5, local copies, waits for them, and re-layouts  8.32 us

profile of v1, /device:TPU:1, one launch (start us, length us, event | category | flops | bytes accessed | tf_op | source)
XLA Modules:
  0.0 115.2 jit_solution(14996460810907711031)
XLA Ops:
  1.3 1.2 %reshape.24.head_w = bf16[1,256]{1,0:T(2,128)(2,1)} reshape(bf16[256]{0:T(256)(128)(2,1)} %param.13) | data formatting | bytes 1024 | tf_op jit(solution)/shard_map/reshape | solution.py:525
  2.5 104.4 %shard_map.119 = (f32[3,256,256]{2,1,0:T(8,128)}, f32[48,256]{1,0:T(8,128)}, f32[3,48,256]{2,1,0:T(8,128)}, f32[3,256,256]{2,1,0:T(8,128)}, f32[1,256]{1,0:T(1,128)}) custom-call(s32[1,4]{1,0:T(1,128)} %spans.1, s32[1]{0:T(128)S(6)} %copy.18.labels, bf16[1024,2048]{1,0:T(8,128)(2,1)} %bitcast.6, bf16[3,256,256]{2,1,0:T(8,128)(2,1)} %conv_w.1, ...), custom_call_target="tpu_custom_call" | custom-call | tf_op jit(solution)/shard_map/pallas_call | solution.py:529
  106.9 2.1 %copy.19 = f32[3,256,256]{2,1,0:T(8,128)} copy(f32[3,256,256]{2,1,0:T(8,128)} %get-tuple-element.20) | data formatting | bytes 1572864
  109.0 1.4 %copy.20 = f32[48,256]{1,0:T(8,128)} copy(f32[48,256]{1,0:T(8,128)} %get-tuple-element.21) | data formatting | bytes 98304
  110.4 1.6 %copy.21 = f32[3,256,48]{1,2,0:T(8,128)} copy(f32[3,256,48]{1,2,0:T(8,128)} %bitcast.7) | data formatting | bytes 294912
  112.0 2.1 %copy.22 = f32[3,256,256]{2,1,0:T(8,128)} copy(f32[3,256,256]{2,1,0:T(8,128)} %get-tuple-element.23) | data formatting | bytes 1572864
  114.0 1.2 %copy.23 = f32[256]{0:T(256)} copy(f32[256]{0:T(256)} %bitcast.9) | data formatting | bytes 2048

commit v2 on v1

--- a/solution.py
+++ b/solution.py
@@ -198,12 +198,20 @@
     return pl.ds(start if isinstance(start, int) else pl.multiple_of(start, height), height * count)
 
 
+def finish_kernel(total1, total2, conv_out, out_out, first_out, second_out, head_out):
+    for part in range(3):
+        conv_out[part] = total2[part].astype(F32)
+        second_out[part] = total1[part, 0:256]
+        first_out[part] = total1[part, 256:304]
+        out_out[16 * part : 16 * part + 16] = total1[part, 304:320]
+    head_out[...] = total1[0, 320:321]
+
+
 def block_kernel(
     loss_scale,
     spans, labels, feat, conv_w, ow, fwt, second_w, head_w,
-    conv_out, out_out, first_out, second_out, head_out,
-    owt, fw, sw, swt, head, total1, total2,
-    frames, hidden, slopes, recon, disc, second, first, parts, rgrad, masked,
+    total1, total2,
+    frames, turned, hidden, slopes, recon, disc, disc_t, second, first, parts, rgrad, conv_t, masked, second_t,
     acc_conv, acc_second, acc_first, acc_out, acc_head, grads1, grads2,
     own_sem, core_send, core_recv, halo_send, halo_recv, low_send, low_recv, high_send, high_recv,
     send1, recv1, send2, recv2, *bufs,
@@ -309,56 +317,59 @@
         frame = 8 * x + local
         return jnp.where((frame >= 0) & (frame < 32), 1.0, 0.0).astype(F32)
 
+    row, column = (lax.broadcasted_iota(jnp.int32, (256, 256), axis) for axis in (0, 1))
+    same = jnp.where(row == column, 1.0, 0.0).astype(jnp.bfloat16)
+    for tap in range(3):
+        block = 256 * (2 - tap)
+        conv_t[block : block + 256] = dot_nt(same, conv_w[tap]).astype(jnp.bfloat16)
+        second_t[256 * tap : 256 * tap + 256] = dot_nt(same, second_w[tap]).astype(jnp.bfloat16)
+
     def mask_weights(local, carry):
-        rows = rows_at(local, 256)
-        for block, tap in ((0, 2), (1, 1)):
-            weight = conv_w[tap].astype(F32) * tap_mask(local, tap)
-            masked[rows, 256 * block : 256 * block + 256] = weight.astype(jnp.bfloat16)
-        masked[rows, 512:768] = conv_w[0]
+        for block, tap in ((0, 2), (1, 1), (2, 0)):
+            weight = conv_t[256 * block : 256 * block + 256].astype(F32) * tap_mask(local, tap)
+            masked[rows_at(3 * local + block, 256)] = weight.astype(jnp.bfloat16)
         return carry
 
-    def place_weights():
-        row, column = (lax.broadcasted_iota(jnp.int32, (256, 256), axis) for axis in (0, 1))
-        same = jnp.where(row == column, 1.0, 0.0).astype(jnp.bfloat16)
-        owt[...] = dot_nt(same, ow[...]).astype(jnp.bfloat16)
-        fw[...] = dot_nt(same, fwt[...]).astype(jnp.bfloat16)
-        for tap in range(3):
-            sw[:, 256 * tap : 256 * tap + 256] = second_w[tap]
-            turned = dot_nt(same, second_w[tap]).astype(jnp.bfloat16)
-            swt[:, 512 - 256 * tap : 768 - 256 * tap] = turned
-        row = jnp.broadcast_to(head_w[...].astype(F32), (256, 256)).astype(jnp.bfloat16)
-        column = dot_nt(same, row)
-        head[...] = jnp.concatenate([column] * (SC // 256), axis=1)
-
     lax.fori_loop(0, 8, mask_weights, 0)
-    place_weights()
     for acc in (acc_conv, acc_second, acc_first, acc_out, acc_head):
         acc[...] = jnp.zeros_like(acc)
 
+    head = head_w[...].astype(F32)
     sign = (2 * labels[0] - 1).astype(F32)
 
-    def decode(local, where):
-        pre = dot(masked[rows_at(local, 256)], frames[rows_at(local, 256, 3), where])
+    def positions(frame, chunk):
+        return slice(frame * WIDTH + chunk * SC, frame * WIDTH + chunk * SC + SC)
+
+    def turn(frame, chunk):
+        turned[positions(frame, chunk)] = frames[rows_at(frame, 256), cols(chunk)].T
+
+    def decode(local, chunk):
+        window = jnp.concatenate([turned[positions(local + tap, chunk)] for tap in range(3)], axis=1)
+        pre = dot(window, masked[rows_at(local, 768)])
         gate = 0.5 * jnp.tanh(0.5 * pre) + 0.5
         silu = pre * gate
-        value = (frames[rows_at(local + 2, 256), where].astype(F32) + silu).astype(jnp.bfloat16)
-        hidden[rows_at(local, 256), where] = value
-        slopes[rows_at(local, 256), where] = gate + silu * (1.0 - gate)
-        recon[rows_at(local + 4, 48), where] = dot(ow[...], value).astype(jnp.bfloat16)
+        value = (turned[positions(local + 2, chunk)].astype(F32) + silu).astype(jnp.bfloat16)
+        hidden[positions(local, chunk)] = value
+        slopes[positions(local, chunk)] = gate + silu * (1.0 - gate)
+        recon[rows_at(local + 4, 48), cols(chunk)] = dot_nt(ow[...], value).astype(jnp.bfloat16)
 
     def decode_inner(chunk):
         own_copy(chunk).wait()
         core_copy(chunk).wait_recv()
-        for local in range(2, 8):
-            decode(local, cols(chunk))
+        for frame in range(2, 10):
+            turn(frame, chunk)
+            if frame >= 4:
+                decode(frame - 2, chunk)
 
     def decode_halo(chunk):
         @pl.when(inner_low)
         def _():
             halo_copy(chunk, 0).wait_recv()
 
-        decode(0, cols(chunk))
-        decode(1, cols(chunk))
+        for frame in (0, 1):
+            turn(frame, chunk)
+        for local in (0, 1):
+            decode(local, chunk)
 
         @pl.when(inner_high)
         def _():
@@ -369,29 +380,36 @@
             high_copy(chunk).start()
 
     def first_layer(local, where):
-        pre = dot(fw[...], recon[rows_at(local + 3, 48, 3), where])
-        on = valid(local)
-        value = pre * jnp.where(pre > 0, on, 0.2 * on)
-        disc[rows_at(local + 3, 256)] = value.astype(jnp.bfloat16)
-
-    def second_layer(local, own):
-        pre = dot(sw[...], disc[rows_at(local + 2, 256, 3)])
+        pre = dot(recon[rows_at(local + 3, 48, 3), where].T, fwt[...])
+        if 0 <= local < 8:
+            value = jnp.maximum(pre, 0.2 * pre)
+        else:
+            on = valid(local)
+            value = pre * jnp.where(pre > 0, on, 0.2 * on)
+        value = value.astype(jnp.bfloat16)
+        disc[rows_at(local + 3, SC)] = value
+        if -1 <= local < 9:
+            disc_t[rows_at(local + 1, 256)] = value.T
+
+    def second_layer(local):
+        window = jnp.concatenate([disc[rows_at(local + 2 + tap, SC)] for tap in range(3)], axis=1)
+        pre = dot(window, second_t[...])
         act = jnp.maximum(pre, 0.2 * pre)
-        logits = jnp.sum(act * head[...], axis=0, keepdims=True)
-        grad = (-sign * loss_scale * valid(local)) / (1.0 + jnp.exp(sign * logits))
-        if own:
-            term = act * grad
-            acc_head[...] += sum(term[:, i : i + 128] for i in range(0, SC, 128))
-        delta = head[...] * grad
-        second[rows_at(local + 2, 256)] = jnp.where(pre > 0, delta, 0.2 * delta).astype(jnp.bfloat16)
+        logits = jnp.sum(act * head, axis=1, keepdims=True)
+        scale = -sign * loss_scale * (1.0 if 0 <= local < 8 else valid(local))
+        grad = scale / (1.0 + jnp.exp(sign * logits))
+        if 0 <= local < 8:
+            acc_head[...] += jnp.sum((act * grad).reshape(SC // 8, 8, 256), axis=0)
+        second[rows_at(local + 2, SC)] = (jnp.where(pre > 0, head, 0.2 * head) * grad).astype(jnp.bfloat16)
 
     def first_back(local):
-        back = dot(swt[...], second[rows_at(local + 1, 256, 3)])
-        on = valid(local)
-        slope = jnp.where(disc[rows_at(local + 3, 256)].astype(F32) > 0, on, 0.2 * on)
+        window = jnp.concatenate([second[rows_at(local + 3 - tap, SC)] for tap in range(3)], axis=1)
+        back = dot(window, second_w[...].reshape(768, 256))
+        on = 1.0 if 0 <= local < 8 else valid(local)
+        slope = jnp.where(disc[rows_at(local + 3, SC)].astype(F32) > 0, on, 0.2 * on)
         value = (back * slope).astype(jnp.bfloat16)
-        first[rows_at(local + 1, 256)] = value
-        parts[rows_at(local + 1, 144)] = dot(fwt[...], value)
+        first[rows_at(local + 1, SC)] = value
+        parts[rows_at(local + 1, 144)] = dot_nt(fwt[...], value)
 
     def recon_back(local, where):
         total = (
@@ -401,20 +419,15 @@
         )
         rgrad[rows_at(local, 48), where] = total.astype(jnp.bfloat16)
 
-    def wide(ref, starts, count, where=slice(None)):
-        return jnp.concatenate([ref[start : start + count, where] for start in starts], axis=1)
-
-    def weight_grads(where):
-        own = range(8)
-        acc_second[...] += dot_nt(
-            wide(disc, [(t + 2) * 256 for t in own], 768), wide(second, [(t + 2) * 256 for t in own], 256)
-        )
-        acc_first[...] += dot_nt(
-            wide(recon, [(t + 3) * 48 for t in own], 144, where), wide(first, [(t + 1) * 256 for t in own], 256)
-        )
-        acc_out[...] += dot_nt(
-            wide(rgrad, [t * 48 for t in own], 48, where), wide(hidden, [t * 256 for t in own], 256, where)
-        )
+    def wide(ref, step, height, where=slice(None)):
+        return jnp.concatenate([ref[start : start + height, where] for start in step], axis=1)
+
+    def weight_grads(chunk):
+        own, where = range(8), cols(chunk)
+        acc_second[...] += dot(wide(disc_t, [t * 256 for t in own], 768), second[2 * SC : 10 * SC])
+        acc_first[...] += dot(wide(recon, [(t + 3) * 48 for t in own], 144, where), first[SC : 9 * SC])
+        value = jnp.concatenate([hidden[positions(t, chunk)] for t in own], axis=0)
+        acc_out[...] += dot(wide(rgrad, [t * 48 for t in own], 48, where), value)
 
     for chunk in range(NCH):
         decode_inner(chunk)
@@ -435,7 +448,7 @@
             if step < 11:
                 first_layer(step, where)
             if -2 <= step - 2 < 10:
-                second_layer(step - 2, 0 <= step - 2 < 8)
+                second_layer(step - 2)
             if -1 <= step - 4 < 9:
                 first_back(step - 4)
             if 0 <= step - 6:
@@ -443,23 +456,23 @@
 
         if chunk + 1 < NCH:
             decode_halo(chunk + 1)
-        weight_grads(where)
+        weight_grads(chunk)
 
     for part in range(3):
         grads1[part, 0:256] = acc_second[256 * part : 256 * part + 256].T
         grads1[part, 256:304] = acc_first[48 * part : 48 * part + 48]
         grads1[part, 304:320] = acc_out[16 * part : 16 * part + 16]
         grads1[part, 320:384] = jnp.zeros((64, 256), F32)
-    grads1[0, 320:328] = jnp.broadcast_to(jnp.sum(acc_head[...].T, axis=0, keepdims=True), (8, 256))
+    grads1[0, 320:328] = jnp.broadcast_to(jnp.sum(acc_head[...], axis=0, keepdims=True), (8, 256))
 
     reduce1 = Reducer(place, grads1, total1, bufs[:6], send1, recv1)
     reduce2 = Reducer(place, grads2, total2, bufs[6:], send2, recv2)
     steps1, steps2 = reduce1.steps(), reduce2.steps()
 
     def conv_back(local):
-        back = dot(owt[...], rgrad[rows_at(local, 48)])
-        delta = (back * slopes[rows_at(local, 256)]).astype(jnp.bfloat16)
-        result = dot_nt(frames[rows_at(local, 256, 3)], delta)
+        back = dot(rgrad[rows_at(local, 48)].T, ow[...])
+        delta = (back * slopes[rows_at(local, WIDTH)]).astype(jnp.bfloat16)
+        result = dot(frames[rows_at(local, 256, 3)], delta)
         for block, tap in ((0, 2), (1, 1), (2, 0)):
             rows = slice(256 * block, 256 * block + 256)
             acc_conv[rows] += result[rows] * tap_mask(local, tap)
@@ -478,13 +491,6 @@
         steps2[index - 3]()
     for index in range(5, 8):
         steps2[index]()
-
-    for part in range(3):
-        conv_out[part] = total2[part].astype(F32)
-        second_out[part] = total1[part, 0:256]
-        first_out[part] = total1[part, 256:304]
-        out_out[16 * part : 16 * part + 16] = total1[part, 304:320]
-    head_out[...] = total1[0, 320:321]
 
     reduce1.finish()
     reduce2.finish()
@@ -526,40 +532,34 @@
     )
     smem, vmem = pl.BlockSpec(memory_space=pltpu.SMEM), pl.BlockSpec(memory_space=pltpu.VMEM)
     dma = pltpu.SemaphoreType.DMA
-    conv, out, first, second, head = pl.pallas_call(
+    totals = pl.pallas_call(
         functools.partial(block_kernel, loss_scale),
         out_shape=(
-            jax.ShapeDtypeStruct((3, 256, 256), F32),
-            jax.ShapeDtypeStruct((48, 256), F32),
-            jax.ShapeDtypeStruct((3, 48, 256), F32),
-            jax.ShapeDtypeStruct((3, 256, 256), F32),
-            jax.ShapeDtypeStruct((1, 256), F32),
+            jax.ShapeDtypeStruct((3, 384, 256), F32),
+            jax.ShapeDtypeStruct((3, 256, 256), bf16),
         ),
         in_specs=[smem, smem, pl.BlockSpec(memory_space=pl.ANY)] + [vmem] * 5,
-        out_specs=(vmem,) * 5,
+        out_specs=(vmem, vmem),
         scratch_shapes=[
-            pltpu.VMEM((256, 48), bf16),
-            pltpu.VMEM((256, 144), bf16),
-            pltpu.VMEM((256, 768), bf16),
-            pltpu.VMEM((256, 768), bf16),
-            pltpu.VMEM((256, SC), F32),
-            pltpu.VMEM((3, 384, 256), F32),
-            pltpu.VMEM((3, 256, 256), bf16),
             pltpu.VMEM((2560, WIDTH), bf16),
-            pltpu.VMEM((2048, WIDTH), bf16),
-            pltpu.VMEM((2048, WIDTH), F32),
+            pltpu.VMEM((10 * WIDTH, 256), bf16),
+            pltpu.VMEM((8 * WIDTH, 256), bf16),
+            pltpu.VMEM((8 * WIDTH, 256), F32),
             pltpu.VMEM((768, WIDTH), bf16),
-            pltpu.VMEM((14 * 256, SC), bf16),
-            pltpu.VMEM((12 * 256, SC), bf16),
+            pltpu.VMEM((14 * SC, 256), bf16),
             pltpu.VMEM((10 * 256, SC), bf16),
+            pltpu.VMEM((12 * SC, 256), bf16),
+            pltpu.VMEM((10 * SC, 256), bf16),
             pltpu.VMEM((10 * 144, SC), F32),
             pltpu.VMEM((8 * 48, WIDTH), bf16),
-            pltpu.VMEM((2048, 768), bf16),
+            pltpu.VMEM((768, 256), bf16),
+            pltpu.VMEM((8 * 768, 256), bf16),
+            pltpu.VMEM((768, 256), bf16),
             pltpu.VMEM((768, 256), F32),
             pltpu.VMEM((768, 256), F32),
             pltpu.VMEM((144, 256), F32),
             pltpu.VMEM((48, 256), F32),
-            pltpu.VMEM((256, 128), F32),
+            pltpu.VMEM((8, 256), F32),
             pltpu.VMEM((3, 384, 256), F32),
             pltpu.VMEM((3, 256, 256), F32),
             dma((NCH,)),
@@ -579,9 +579,22 @@
         + reduce_scratch(384)
         + reduce_scratch(256),
         compiler_params=pltpu.CompilerParams(
-            collective_id=0, has_side_effects=True, vmem_limit_bytes=56 * MIB
+            collective_id=0, has_side_effects=True, vmem_limit_bytes=58 * MIB
         ),
     )(*operands)
+    conv, out, first, second, head = pl.pallas_call(
+        finish_kernel,
+        out_shape=(
+            jax.ShapeDtypeStruct((3, 256, 256), F32),
+            jax.ShapeDtypeStruct((48, 256), F32),
+            jax.ShapeDtypeStruct((3, 48, 256), F32),
+            jax.ShapeDtypeStruct((3, 256, 256), F32),
+            jax.ShapeDtypeStruct((1, 256), F32),
+        ),
+        in_specs=[vmem, vmem],
+        out_specs=(vmem,) * 5,
+        compiler_params=pltpu.CompilerParams(vmem_limit_bytes=16 * MIB),
+    )(*totals)
     return conv, out, jnp.swapaxes(first, 1, 2), second, head.reshape(256)
 
 

time: 116 us -> 108 us (0.931)
  local copies, waits for them, and re-layouts: 9.55 us -> 3.48 us
    unnamed x5 -> x4, local copies, waits for them, and re-layouts: 8.32 us -> 2.26 us
    pallas_call x1, Pallas kernels: 104 us -> 102 us  [per_device(): pl.pallas_call(functools.partial(block_kernel, loss_scale), out_shape=(ja...]
    pallas_call x0 -> x1, Pallas kernels: none -> 1.32 us  [per_device(): pl.pallas_call(finish_kernel, out_shape=(jax.ShapeDtypeStruct((3, 256, 25...]
where the time goes in v2:
time: 108 us
  Pallas kernels  103 us (95%)
  local copies, waits for them, and re-layouts  3.48 us (3%)
  between operations  1.3 us (1%)
    pallas_call x1, Pallas kernels, per_device(): pl.pallas_call(functools.partial(block_kernel, loss_scale), out_shape=(ja...  102 us
    unnamed x4, local copies, waits for them, and re-layouts  2.26 us

profile of v2, /device:TPU:1, one launch (start us, length us, event | category | flops | bytes accessed | tf_op | source)
XLA Modules:
  0.0 108.0 jit_solution(9782010071294233560)
XLA Ops:
  1.3 1.2 %reshape.24.head_w = bf16[1,256]{1,0:T(2,128)(2,1)} reshape(bf16[256]{0:T(256)(128)(2,1)} %param.13) | data formatting | bytes 1024 | tf_op jit(solution)/shard_map/reshape | solution.py:531
  2.5 101.9 %shard_map.119 = (f32[3,384,256]{2,1,0:T(8,128)}, bf16[3,256,256]{2,1,0:T(8,128)(2,1)}) custom-call(s32[1,4]{1,0:T(1,128)} %spans.1, s32[1]{0:T(128)S(6)} %copy.13.labels, bf16[1024,2048]{1,0:T(8,128)(2,1)} %bitcast.6, bf16[3,256,256]{2,1,0:T(8,128)(2,1)} %conv_w.1, bf16[48,256]{1,0:T(8,128)(2,1)} %ow.1, bf16[144,256]{1,0:T(8,128)(2,1)} %bitcast.7, ...), custom_call_target="tpu_custom_call" | custom-call | tf_op jit(solution)/shard_map/pallas_call | solution.py:535
  104.4 0.0 copy-start
  104.4 1.3 %copy-done = f32[3,384,256]{2,1,0:T(8,128)S(1)} copy-done((f32[3,384,256]{2,1,0:T(8,128)S(1)}, f32[3,384,256]{2,1,0:T(8,128)}, u32[]{:S(2)}) %copy-start) | copy-done | bytes 1179672
  105.7 0.0 copy-start.1
  105.7 1.0 copy-done.1
  106.7 1.3 %shard_map.120 = (f32[3,256,256]{2,1,0:T(8,128)}, f32[48,256]{1,0:T(8,128)}, f32[3,48,256]{2,1,0:T(8,128)}, f32[3,256,256]{2,1,0:T(8,128)}, f32[1,256]{1,0:T(1,128)}) custom-call(f32[3,384,256]{2,1,0:T(8,128)S(1)} %copy-done, bf16[3,256,256]{2,1,0:T(8,128)(2,1)S(1)} %copy-done.1), custom_call_target="tpu_custom_call" | custom-call | tf_op jit(solution)/shard_map/pallas_call | solution.py:585
Async XLA Ops:
  104.4 1.3 %copy-start = (f32[3,384,256]{2,1,0:T(8,128)S(1)}, f32[3,384,256]{2,1,0:T(8,128)}, u32[]{:S(2)}) copy-start(f32[3,384,256]{2,1,0:T(8,128)} %get-tuple-element.12.total1) | copy-start | bytes 3538948
  105.7 1.0 copy-start.1

commit v3 on v2

--- a/solution.py
+++ b/solution.py
@@ -32,7 +32,7 @@
 class Reducer:
     def __init__(self, place, grads, total, bufs, send_sems, recv_sems):
         self.place, self.grads, self.total = (place, grads, total)
-        self.core_in, self.sum1, self.in1, self.sum2, self.in2, self.in3 = bufs
+        self.sum1, self.in1, self.sum2, self.in2, self.in3 = bufs
         self.send_sems, self.recv_sems = (send_sems, recv_sems)
         self.rows = grads.shape[1]
         self.sent = []
@@ -65,12 +65,12 @@
     def core_send(self, part):
         place = self.place
         src = self.grads.at[part, :, self.lanes(1 - place.core)]
-        self.start(src, self.core_in.at[part], part, place.other_core())
+        self.start(src, self.sum1.at[part], part, place.other_core())
 
     def core_sum(self, part):
         place = self.place
-        self.copy(self.core_in.at[part], self.core_in.at[part], part, place.other_core()).wait_recv()
-        self.sum1[part] = self.grads[part, :, self.lanes(place.core)] + self.core_in[part]
+        self.copy(self.sum1.at[part], self.sum1.at[part], part, place.other_core()).wait_recv()
+        self.sum1[part] = self.grads[part, :, self.lanes(place.core)] + self.sum1[part]
 
     def scatter_send(self, part, level):
         axis = self.axes[part][level]
@@ -171,7 +171,6 @@
 def reduce_scratch(rows):
     return [
         pltpu.VMEM((3, rows, 128), F32),
-        pltpu.VMEM((3, rows, 128), F32),
         pltpu.VMEM((3, 3, rows // 4, 128), F32),
         pltpu.VMEM((3, rows // 4, 128), F32),
         pltpu.VMEM((3, 3, rows // 16, 128), F32),
@@ -211,9 +210,10 @@
     loss_scale,
     spans, labels, feat, conv_w, ow, fwt, second_w, head_w,
     total1, total2,
-    frames, turned, hidden, slopes, recon, disc, disc_t, second, first, parts, rgrad, conv_t, masked, second_t,
+    frames, turned, hidden, slopes, recon, disc, disc_t, second, first, parts, rgrad, conv_t, second_t,
     acc_conv, acc_second, acc_first, acc_out, acc_head, grads1, grads2,
-    own_sem, core_send, core_recv, halo_send, halo_recv, low_send, low_recv, high_send, high_recv,
+    own_sem, core_send, core_recv, after_send, after_recv, before_send, before_recv,
+    low_send, low_recv, high_send, high_recv,
     send1, recv1, send2, recv2, *bufs,
 ):
     place = Place()
@@ -228,7 +228,7 @@
     def own_copy(chunk):
         return pltpu.make_async_copy(
             feat.at[:, cols(chunk, core * WIDTH)],
-            frames.at[rows_at(2 + 4 * core, 256, 4), cols(chunk)],
+            frames.at[chunk, rows_at(1 + 4 * core, 256, 4)],
             own_sem.at[chunk],
         )
 
@@ -240,25 +240,34 @@
     def core_copy(chunk):
         return remote(
             feat.at[:, cols(chunk, (1 - core) * WIDTH)],
-            frames.at[rows_at(2 + 4 * core, 256, 4), cols(chunk)],
+            frames.at[chunk, rows_at(1 + 4 * core, 256, 4)],
             core_send.at[chunk],
             core_recv.at[chunk],
             place.other_core(),
         )
 
-    def halo_copy(chunk, target):
+    def after_copy(chunk):
         return remote(
-            feat.at[512:1024, cols(chunk, target * WIDTH)],
-            frames.at[0:512, cols(chunk)],
-            halo_send.at[chunk, target],
-            halo_recv.at[chunk],
-            place.device(x + 1, y, z, target),
+            frames.at[chunk, 2048:2304],
+            frames.at[chunk, 0:256],
+            after_send.at[chunk],
+            after_recv.at[chunk],
+            place.device(x + 1, y, z, core),
+        )
+
+    def before_copy(chunk):
+        return remote(
+            frames.at[chunk, 256:512],
+            frames.at[chunk, 2304:2560],
+            before_send.at[chunk],
+            before_recv.at[chunk],
+            place.device(x - 1, y, z, core),
         )
 
     def low_copy(chunk):
         return remote(
-            recon.at[384:576, cols(chunk)],
-            recon.at[0:192, cols(chunk)],
+            recon.at[chunk, 384:576],
+            recon.at[chunk, 0:192],
             low_send.at[chunk],
             low_recv.at[chunk],
             place.device(x + 1, y, z, core),
@@ -266,19 +275,39 @@
 
     def high_copy(chunk):
         return remote(
-            recon.at[192:384, cols(chunk)],
-            recon.at[576:768, cols(chunk)],
+            recon.at[chunk, 192:384],
+            recon.at[chunk, 576:768],
             high_send.at[chunk],
             high_recv.at[chunk],
             place.device(x - 1, y, z, core),
         )
 
+    def to_both_sides(up, down, act):
+        @pl.when(inner_high)
+        def _():
+            act(up)
+
+        @pl.when(inner_low)
+        def _():
+            act(down)
+
+    def send_halo(chunk):
+        to_both_sides(after_copy(chunk), before_copy(chunk), lambda copy: copy.start())
+
+    def await_halo(chunk):
+        to_both_sides(before_copy(chunk), after_copy(chunk), lambda copy: copy.wait_recv())
+
+    def send_recon(chunk):
+        to_both_sides(low_copy(chunk), high_copy(chunk), lambda copy: copy.start())
+
+    def await_recon(chunk):
+        to_both_sides(high_copy(chunk), low_copy(chunk), lambda copy: copy.wait_recv())
+
     for chunk in range(NCH):
         own_copy(chunk).start()
 
     barrier = pltpu.get_barrier_semaphore()
     partners = [place.other_core()] + [place.along(axis, step) for axis in range(3) for step in (1, 2, 3)]
-    partners += [place.device(lax.rem(x + step, 4), y, z, 1 - core) for step in (1, 3)]
     for device in partners:
         pl.semaphore_signal(barrier, inc=1, device_id=device, device_id_type=MESH)
     pl.semaphore_wait(barrier, len(partners))
@@ -286,20 +315,17 @@
     for chunk in range(NCH):
         core_copy(chunk).start()
 
-    @pl.when((core == 1) & inner_high)
+    @pl.when(clip_start)
     def _():
         for chunk in range(NCH):
-            for target in (0, 1):
-                halo_copy(chunk, target).start()
-
-    @pl.when(clip_start)
-    def _():
-        frames[0:512] = jnp.zeros((512, WIDTH), jnp.bfloat16)
-        recon[0:192] = jnp.zeros((192, WIDTH), jnp.bfloat16)
+            frames[chunk, 0:256] = jnp.zeros((256, SC), jnp.bfloat16)
+            recon[chunk, 0:192] = jnp.zeros((192, SC), jnp.bfloat16)
 
     @pl.when(clip_end)
     def _():
-        recon[576:768] = jnp.zeros((192, WIDTH), jnp.bfloat16)
+        for chunk in range(NCH):
+            frames[chunk, 2304:2560] = jnp.zeros((256, SC), jnp.bfloat16)
+            recon[chunk, 576:768] = jnp.zeros((192, SC), jnp.bfloat16)
 
     ends = []
     for span in range(4):
@@ -309,12 +335,12 @@
         return sum((frame >= end).astype(jnp.int32) for end in ends)
 
     def tap_mask(local, tap):
-        frame = 8 * x + local
-        same = (span_of(frame) == span_of(frame - tap)) & (frame >= tap)
+        frame = 8 * x + 1 + local
+        same = (span_of(frame) == span_of(frame - tap)) & (frame >= tap) & (frame < 32)
         return jnp.where(same, 1.0, 0.0).astype(F32)
 
     def valid(local):
-        frame = 8 * x + local
+        frame = 8 * x + 1 + local
         return jnp.where((frame >= 0) & (frame < 32), 1.0, 0.0).astype(F32)
 
     row, column = (lax.broadcasted_iota(jnp.int32, (256, 256), axis) for axis in (0, 1))
@@ -324,13 +350,6 @@
         conv_t[block : block + 256] = dot_nt(same, conv_w[tap]).astype(jnp.bfloat16)
         second_t[256 * tap : 256 * tap + 256] = dot_nt(same, second_w[tap]).astype(jnp.bfloat16)
 
-    def mask_weights(local, carry):
-        for block, tap in ((0, 2), (1, 1), (2, 0)):
-            weight = conv_t[256 * block : 256 * block + 256].astype(F32) * tap_mask(local, tap)
-            masked[rows_at(3 * local + block, 256)] = weight.astype(jnp.bfloat16)
-        return carry
-
-    lax.fori_loop(0, 8, mask_weights, 0)
     for acc in (acc_conv, acc_second, acc_first, acc_out, acc_head):
         acc[...] = jnp.zeros_like(acc)
 
@@ -341,47 +360,51 @@
         return slice(frame * WIDTH + chunk * SC, frame * WIDTH + chunk * SC + SC)
 
     def turn(frame, chunk):
-        turned[positions(frame, chunk)] = frames[rows_at(frame, 256), cols(chunk)].T
+        turned[positions(frame, chunk)] = frames[chunk, rows_at(frame, 256)].T
+
+    def activate(pre, center, slot, recon_slot, chunk):
+        gate = 0.5 * jnp.tanh(0.5 * pre) + 0.5
+        silu = pre * gate
+        value = (turned[positions(center, chunk)].astype(F32) + silu).astype(jnp.bfloat16)
+        hidden[positions(slot, chunk)] = value
+        slopes[positions(slot, chunk)] = gate + silu * (1.0 - gate)
+        recon[chunk, rows_at(recon_slot, 48)] = dot_nt(ow[...], value).astype(jnp.bfloat16)
 
     def decode(local, chunk):
         window = jnp.concatenate([turned[positions(local + tap, chunk)] for tap in range(3)], axis=1)
-        pre = dot(window, masked[rows_at(local, 768)])
-        gate = 0.5 * jnp.tanh(0.5 * pre) + 0.5
-        silu = pre * gate
-        value = (turned[positions(local + 2, chunk)].astype(F32) + silu).astype(jnp.bfloat16)
-        hidden[positions(local, chunk)] = value
-        slopes[positions(local, chunk)] = gate + silu * (1.0 - gate)
-        recon[rows_at(local + 4, 48), cols(chunk)] = dot_nt(ow[...], value).astype(jnp.bfloat16)
-
-    def decode_inner(chunk):
+        weight = [
+            conv_t[256 * block : 256 * block + 256]
+            * jnp.full((1, 256), tap_mask(local, 2 - block), F32).astype(jnp.bfloat16)
+            for block in range(3)
+        ]
+        pre = dot(window, jnp.concatenate(weight, axis=0))
+        activate(pre, local + 2, local, local + 4, chunk)
+
+    def await_frames(chunk):
         own_copy(chunk).wait()
         core_copy(chunk).wait_recv()
-        for frame in range(2, 10):
+
+    def decode_inner(chunk):
+        for frame in range(1, 9):
             turn(frame, chunk)
-            if frame >= 4:
+            if frame >= 3:
                 decode(frame - 2, chunk)
 
+        @pl.when(clip_start)
+        def _():
+            activate(dot(turned[positions(1, chunk)], conv_t[512:768]), 1, 8, 3, chunk)
+
     def decode_halo(chunk):
-        @pl.when(inner_low)
-        def _():
-            halo_copy(chunk, 0).wait_recv()
-
-        for frame in (0, 1):
+        await_halo(chunk)
+        for frame in (0, 9):
             turn(frame, chunk)
-        for local in (0, 1):
+        for local in (0, 7):
             decode(local, chunk)
-
-        @pl.when(inner_high)
-        def _():
-            low_copy(chunk).start()
-
-        @pl.when(inner_low)
-        def _():
-            high_copy(chunk).start()
-
-    def first_layer(local, where):
-        pre = dot(recon[rows_at(local + 3, 48, 3), where].T, fwt[...])
-        if 0 <= local < 8:
+        send_recon(chunk)
+
+    def first_layer(local, chunk):
+        pre = dot(recon[chunk, rows_at(local + 3, 48, 3)].T, fwt[...])
+        if 0 <= local < 7:
             value = jnp.maximum(pre, 0.2 * pre)
         else:
             on = valid(local)
@@ -396,16 +419,17 @@
         pre = dot(window, second_t[...])
         act = jnp.maximum(pre, 0.2 * pre)
         logits = jnp.sum(act * head, axis=1, keepdims=True)
-        scale = -sign * loss_scale * (1.0 if 0 <= local < 8 else valid(local))
+        scale = -sign * loss_scale * (1.0 if 0 <= local < 7 else valid(local))
         grad = scale / (1.0 + jnp.exp(sign * logits))
-        if 0 <= local < 8:
-            acc_head[...] += jnp.sum((act * grad).reshape(SC // 8, 8, 256), axis=0)
+        if -1 <= local < 8:
+            share = grad * jnp.where(clip_start, 1.0, 0.0).astype(F32) if local < 0 else grad
+            acc_head[...] += jnp.sum((act * share).reshape(SC // 8, 8, 256), axis=0)
         second[rows_at(local + 2, SC)] = (jnp.where(pre > 0, head, 0.2 * head) * grad).astype(jnp.bfloat16)
 
     def first_back(local):
         window = jnp.concatenate([second[rows_at(local + 3 - tap, SC)] for tap in range(3)], axis=1)
         back = dot(window, second_w[...].reshape(768, 256))
-        on = 1.0 if 0 <= local < 8 else valid(local)
+        on = 1.0 if 0 <= local < 7 else valid(local)
         slope = jnp.where(disc[rows_at(local + 3, SC)].astype(F32) > 0, on, 0.2 * on)
         value = (back * slope).astype(jnp.bfloat16)
         first[rows_at(local + 1, SC)] = value
@@ -419,41 +443,50 @@
         )
         rgrad[rows_at(local, 48), where] = total.astype(jnp.bfloat16)
 
-    def wide(ref, step, height, where=slice(None)):
-        return jnp.concatenate([ref[start : start + height, where] for start in step], axis=1)
+    def recon_back_first(where):
+        rgrad[rows_at(8, 48), where] = (parts[144:192] + parts[48:96]).astype(jnp.bfloat16)
+
+    def wide(blocks):
+        return jnp.concatenate(blocks, axis=1)
 
     def weight_grads(chunk):
         own, where = range(8), cols(chunk)
-        acc_second[...] += dot(wide(disc_t, [t * 256 for t in own], 768), second[2 * SC : 10 * SC])
-        acc_first[...] += dot(wide(recon, [(t + 3) * 48 for t in own], 144, where), first[SC : 9 * SC])
+        left = wide([disc_t[t * 256 : t * 256 + 768] for t in own])
+        acc_second[...] += dot(left, second[2 * SC : 10 * SC])
+        left = wide([recon[chunk, (t + 3) * 48 : (t + 6) * 48] for t in own])
+        acc_first[...] += dot(left, first[SC : 9 * SC])
         value = jnp.concatenate([hidden[positions(t, chunk)] for t in own], axis=0)
-        acc_out[...] += dot(wide(rgrad, [t * 48 for t in own], 48, where), value)
-
-    for chunk in range(NCH):
+        acc_out[...] += dot(wide([rgrad[t * 48 : t * 48 + 48, where] for t in own]), value)
+
+        @pl.when(clip_start)
+        def _():
+            acc_second[256:768] += dot(disc_t[0:512], second[SC : 2 * SC])
+            acc_first[48:144] += dot(recon[chunk, 144:240], first[0:SC])
+            acc_out[...] += dot(rgrad[384:432, where], hidden[positions(8, chunk)])
+
+    await_frames(0)
+    send_halo(0)
+    decode_inner(0)
+    decode_halo(0)
+    for chunk in range(1, NCH):
+        await_frames(chunk)
         decode_inner(chunk)
-    decode_halo(0)
 
     for chunk in range(NCH):
         where = cols(chunk)
-
-        @pl.when(inner_low)
-        def _():
-            low_copy(chunk).wait_recv()
-
-        @pl.when(inner_high)
-        def _():
-            high_copy(chunk).wait_recv()
-
+        await_recon(chunk)
+        if chunk + 1 < NCH:
+            send_halo(chunk + 1)
         for step in range(-3, 14):
             if step < 11:
-                first_layer(step, where)
+                first_layer(step, chunk)
             if -2 <= step - 2 < 10:
                 second_layer(step - 2)
             if -1 <= step - 4 < 9:
                 first_back(step - 4)
             if 0 <= step - 6:
                 recon_back(step - 6, where)
-
+        recon_back_first(where)
         if chunk + 1 < NCH:
             decode_halo(chunk + 1)
         weight_grads(chunk)
@@ -465,19 +498,25 @@
         grads1[part, 320:384] = jnp.zeros((64, 256), F32)
     grads1[0, 320:328] = jnp.broadcast_to(jnp.sum(acc_head[...], axis=0, keepdims=True), (8, 256))
 
-    reduce1 = Reducer(place, grads1, total1, bufs[:6], send1, recv1)
-    reduce2 = Reducer(place, grads2, total2, bufs[6:], send2, recv2)
+    reduce1 = Reducer(place, grads1, total1, bufs[:5], send1, recv1)
+    reduce2 = Reducer(place, grads2, total2, bufs[5:], send2, recv2)
     steps1, steps2 = reduce1.steps(), reduce2.steps()
 
     def conv_back(local):
         back = dot(rgrad[rows_at(local, 48)].T, ow[...])
         delta = (back * slopes[rows_at(local, WIDTH)]).astype(jnp.bfloat16)
-        result = dot(frames[rows_at(local, 256, 3)], delta)
+        result = dot(wide([frames[chunk, rows_at(local, 256, 3)] for chunk in range(NCH)]), delta)
         for block, tap in ((0, 2), (1, 1), (2, 0)):
             rows = slice(256 * block, 256 * block + 256)
             acc_conv[rows] += result[rows] * tap_mask(local, tap)
 
+    def conv_back_first():
+        back = dot(rgrad[rows_at(8, 48)].T, ow[...])
+        delta = (back * slopes[rows_at(8, WIDTH)]).astype(jnp.bfloat16)
+        acc_conv[512:768] += dot(wide([frames[chunk, 256:512] for chunk in range(NCH)]), delta)
+
     steps1[0]()
+    pl.when(clip_start)(conv_back_first)
     for pair in range(4):
         conv_back(2 * pair)
         conv_back(2 * pair + 1)
@@ -497,18 +536,8 @@
     for chunk in range(NCH):
         core_copy(chunk).wait_send()
 
-        @pl.when((core == 1) & inner_high)
-        def _():
-            halo_copy(chunk, 0).wait_send()
-            halo_copy(chunk, 1).wait_send()
-
-        @pl.when(inner_high)
-        def _():
-            low_copy(chunk).wait_send()
-
-        @pl.when(inner_low)
-        def _():
-            high_copy(chunk).wait_send()
+        to_both_sides(after_copy(chunk), before_copy(chunk), lambda copy: copy.wait_send())
+        to_both_sides(low_copy(chunk), high_copy(chunk), lambda copy: copy.wait_send())
 
 
 def per_device(
@@ -541,19 +570,18 @@
         in_specs=[smem, smem, pl.BlockSpec(memory_space=pl.ANY)] + [vmem] * 5,
         out_specs=(vmem, vmem),
         scratch_shapes=[
-            pltpu.VMEM((2560, WIDTH), bf16),
+            pltpu.VMEM((NCH, 2560, SC), bf16),
             pltpu.VMEM((10 * WIDTH, 256), bf16),
-            pltpu.VMEM((8 * WIDTH, 256), bf16),
-            pltpu.VMEM((8 * WIDTH, 256), F32),
-            pltpu.VMEM((768, WIDTH), bf16),
+            pltpu.VMEM((9 * WIDTH, 256), bf16),
+            pltpu.VMEM((9 * WIDTH, 256), F32),
+            pltpu.VMEM((NCH, 768, SC), bf16),
             pltpu.VMEM((14 * SC, 256), bf16),
             pltpu.VMEM((10 * 256, SC), bf16),
             pltpu.VMEM((12 * SC, 256), bf16),
             pltpu.VMEM((10 * SC, 256), bf16),
             pltpu.VMEM((10 * 144, SC), F32),
-            pltpu.VMEM((8 * 48, WIDTH), bf16),
+            pltpu.VMEM((9 * 48, WIDTH), bf16),
             pltpu.VMEM((768, 256), bf16),
-            pltpu.VMEM((8 * 768, 256), bf16),
             pltpu.VMEM((768, 256), bf16),
             pltpu.VMEM((768, 256), F32),
             pltpu.VMEM((768, 256), F32),
@@ -565,7 +593,9 @@
             dma((NCH,)),
             dma((NCH,)),
             dma((NCH,)),
-            dma((NCH, 2)),
+            dma((NCH,)),
+            dma((NCH,)),
+            dma((NCH,)),
             dma((NCH,)),
             dma((NCH,)),
             dma((NCH,)),

time: 108 us -> 96.9 us (0.90)
  Pallas kernels: 103 us -> 91.9 us
    pallas_call x1, Pallas kernels: 102 us -> 90.6 us  [per_device(): pl.pallas_call(functools.partial(block_kernel, loss_scale), out_shape=(ja...]
where the time goes in v3:
time: 96.9 us; the launch traced here: 96.7 us
  Pallas kernels  91.9 us (95%)
  local copies, waits for them, and re-layouts  3.48 us (4%)
  between operations  1.3 us (1%)
    pallas_call x1, Pallas kernels, per_device(): pl.pallas_call(functools.partial(block_kernel, loss_scale), out_shape=(ja...  90.6 us
    unnamed x4, local copies, waits for them, and re-layouts  2.26 us

profile of v3, /device:TPU:1, one launch (start us, length us, event | category | flops | bytes accessed | tf_op | source)
XLA Modules:
  0.0 96.7 jit_solution(8288019573261580977)
XLA Ops:
  1.3 1.2 %reshape.24.head_w = bf16[1,256]{1,0:T(2,128)(2,1)} reshape(bf16[256]{0:T(256)(128)(2,1)} %param.13) | data formatting | bytes 1024 | tf_op jit(solution)/shard_map/reshape | solution.py:560
  2.5 90.6 %shard_map.119 = (f32[3,384,256]{2,1,0:T(8,128)}, bf16[3,256,256]{2,1,0:T(8,128)(2,1)}) custom-call(s32[1,4]{1,0:T(1,128)} %spans.1, s32[1]{0:T(128)S(6)} %copy.13.labels, bf16[1024,2048]{1,0:T(8,128)(2,1)} %bitcast.6, bf16[3,256,256]{2,1,0:T(8,128)(2,1)} %conv_w.1, bf16[48,256]{1,0:T(8,128)(2,1)} %ow.1, bf16[144,256]{1,0:T(8,128)(2,1)} %bitcast.7, ...), custom_call_target="tpu_custom_call" | custom-call | tf_op jit(solution)/shard_map/pallas_call | solution.py:564
  93.1 0.0 copy-start
  93.1 1.3 %copy-done = f32[3,384,256]{2,1,0:T(8,128)S(1)} copy-done((f32[3,384,256]{2,1,0:T(8,128)S(1)}, f32[3,384,256]{2,1,0:T(8,128)}, u32[]{:S(2)}) %copy-start) | copy-done | bytes 1179672
  94.4 0.0 copy-start.1
  94.4 1.0 %copy-done.1 = bf16[3,256,256]{2,1,0:T(8,128)(2,1)S(1)} copy-done((bf16[3,256,256]{2,1,0:T(8,128)(2,1)S(1)}, bf16[3,256,256]{2,1,0:T(8,128)(2,1)}, u32[]{:S(2)}) %copy-start.1) | copy-done | bytes 393240
  95.4 1.3 %shard_map.120 = (f32[3,256,256]{2,1,0:T(8,128)}, f32[48,256]{1,0:T(8,128)}, f32[3,48,256]{2,1,0:T(8,128)}, f32[3,256,256]{2,1,0:T(8,128)}, f32[1,256]{1,0:T(1,128)}) custom-call(f32[3,384,256]{2,1,0:T(8,128)S(1)} %copy-done, bf16[3,256,256]{2,1,0:T(8,128)(2,1)S(1)} %copy-done.1), custom_call_target="tpu_custom_call" | custom-call | tf_op jit(solution)/shard_map/pallas_call | solution.py:615
Async XLA Ops:
  93.1 1.3 %copy-start = (f32[3,384,256]{2,1,0:T(8,128)S(1)}, f32[3,384,256]{2,1,0:T(8,128)}, u32[]{:S(2)}) copy-start(f32[3,384,256]{2,1,0:T(8,128)} %get-tuple-element.12.total1) | copy-start | bytes 3538948
  94.4 1.0 %copy-start.1 = (bf16[3,256,256]{2,1,0:T(8,128)(2,1)S(1)}, bf16[3,256,256]{2,1,0:T(8,128)(2,1)}, u32[]{:S(2)}) copy-start(bf16[3,256,256]{2,1,0:T(8,128)(2,1)} %get-tuple-element.13.total2) | copy-start | bytes 1179652
